TPU v7x, 32 devices: a whole 2x2x4 slice. The times are simulated.
32 devices in a mesh: pair: 4 (over x, core), ints: 8 (over z, y).
Axes of the slice: x: 2, y: 2, z: 4, core: 2. Of those that a mesh axis runs over, the one named last changes fastest.
Arguments:
- t2: bfloat16 [2048, 4096], P('pair', 'ints'), may hold values from -6 to 6
- t2_live: int32 [4, 32], P('pair', 'ints'), may hold values 0 or 1
- int_tiles: int32 [2560, 2], P('ints'), may hold values from 0 to 31
- integrals: bfloat16 [2560, 128, 128], P('ints'), may hold values from -0.0625 to 0.0625
- cycle_w: bfloat16 [2048, 2048], P('pair'), may hold values from -0.125 to 0.125
- res_live: int32 [4, 32], P('pair', 'ints'), may hold values 0 or 1
Outputs:
- residual: float32 [2048, 4096], P('pair', 'ints')
All inputs are finite; a program needn't handle non-finite values. No bound on the sum of `t2_live` or of `res_live` on one device may be relied on, other than what follows from the above.
Results may differ from a plain program's by a relative error of at most 0.0003.
Values may be sent and summed in bfloat16 or wider, within the bound.
A program may use at most 192 MiB of HBM per device.

v0:
```python
import jax
import jax.numpy as jnp
from jax import lax
from jax.sharding import PartitionSpec as P


def local(t2, t2_live, int_tiles, integrals, cycle_w, res_live):
    rows_here = t2.shape[0]
    tile_size = integrals.shape[1]
    tiles_here = t2.shape[1] // tile_size
    live_mask = t2_live[0].astype(t2.dtype)
    amps = (t2.reshape(rows_here, tiles_here, tile_size) * live_mask[None, :, None]).reshape(
        rows_here, tiles_here * tile_size
    )
    block_amps = lax.all_gather(amps, "ints", axis=1, tiled=True)
    tiles_all = block_amps.shape[1] // tile_size
    amps_tiled = block_amps.reshape(rows_here, tiles_all, tile_size)
    count_here = integrals.shape[0]
    group_size = 64
    tile_groups = int_tiles.reshape(count_here // group_size, group_size, 2)
    int_groups = integrals.reshape(count_here // group_size, group_size, tile_size, tile_size)
    tile_ids = jnp.arange(tiles_all, dtype=jnp.int32)

    def ladder_step(partial_value, entry):
        pairs_uv, blocks = entry
        source_table = (pairs_uv[:, 0:1] == tile_ids[None, :]).astype(jnp.bfloat16)
        target_table = (pairs_uv[:, 1:2] == tile_ids[None, :]).astype(jnp.float32)
        picked = jnp.einsum(
            "jt,ptc->jpc", source_table, amps_tiled, preferred_element_type=jnp.float32
        ).astype(jnp.bfloat16)
        product = jnp.einsum("jpc,jcd->jpd", picked, blocks, preferred_element_type=jnp.float32)
        partial_value = partial_value + jnp.einsum(
            "jv,jpd->vpd", target_table, product, precision=lax.Precision.HIGHEST
        )
        return (partial_value, None)

    start_sum = jnp.zeros((tiles_all, rows_here, tile_size), jnp.float32)
    partial_value, _ = lax.scan(ladder_step, start_sum, (tile_groups, int_groups))
    summed = lax.psum(partial_value, "ints")
    owned = lax.dynamic_slice_in_dim(summed, lax.axis_index("ints") * tiles_here, tiles_here, 0)
    ladder = owned.transpose(1, 0, 2).reshape(rows_here, tiles_here * tile_size)
    cycle_term = jnp.dot(
        cycle_w,
        lax.all_gather(amps, "pair", axis=0, tiled=True),
        preferred_element_type=jnp.float32,
    )
    keep_mask = jnp.repeat(res_live[0], tile_size).astype(jnp.float32)[None, :]
    return keep_mask * (ladder + cycle_term)


def solution(mesh):
    placed = (
        P("pair", "ints"),
        P("pair", "ints"),
        P("ints", None),
        P("ints", None, None),
        P("pair", None),
        P("pair", "ints"),
    )
    return jax.shard_map(
        local, mesh=mesh, in_specs=placed, out_specs=P("pair", "ints"), check_vma=False
    )
```

profile of v0, /device:TPU:0, one launch (start us, length us, event | category | flops | bytes accessed | tf_op | source)
XLA Modules:
  0.0 627.7 jit_solution(13638411692792028920)
XLA Ops:
  7.4 0.0 copy-start
  7.4 0.0 all-gather.3.cloned.1.call-start
  7.4 0.8 convert_bitcast_fusion
  8.2 0.1 broadcast_bitcast_fusion.1
  8.3 1.9 broadcast_multiply_fusion
  10.1 0.0 all-gather.3.cloned.1.call-update
  10.2 0.0 all-reduce.2.cloned.1.call-start
  10.2 0.8 reshape.30
  11.0 77.0 %all-gather.3.cloned.1.call-done = bf16[512,4096]{1,0:T(8,128)(2,1)} async-done(((bf16[512,512]{1,0:T(8,128)(2,1)}), bf16[512,4096]{1,0:T(8,128)(2,1)}) %all-gather.3.cloned.1.call-update) | async-done | bytes 4194320 | tf_op jit(solution)/shard_map/all_gather | solution.py:15
  88.0 5.5 copy.15
  93.6 250.4 %while.12 = (s32[]{:T(128)}, f32[32,512,128]{2,0,1:T(8,128)}, s32[5,64,2]{1,0,2:T(8,128)S(1)}, bf16[512,32,128]{2,1,0:T(8,128)(2,1)}, bf16[5,64,128,128]{3,2,1,0:T(8,128)(2,1)}, /*index=5*/s32[]{:T(128)}, s32[]{:T(128)}) while((s32[]{:T(128)}, f32[32,512,128]{2,0,1:T(8,128)}, s32[5,64,2]{1,0,2:T(8,128)S(1)}, ...), condition=%wide.region_1.2_spmd.clone.clone, body=%wide.region_0.1_spmd.clone.clone.sunk | while | flops 2956988416 | bytes 73403480 | solution.py:38
  93.6 7.8 %fusion.34 = bf16[64,512,128]{2,0,1:T(8,128)(2,1)} fusion(bf16[512,32,128]{2,1,0:T(8,128)(2,1)} %get-tuple-element.146, s32[64]{0:T(128)S(1)} %get-tuple-element.127), kind=kOutput, calls=%fused_computation.12.clone.1 | convolution fusion | flops 268437504 | bytes 12583168 | tf_op jit(solution)/shard_map/while/body/eval_jaxpr/jt,ptc->jpc/dot_general | solution.py:28
  101.4 18.1 %fusion.35 = f32[64,512,128]{2,1,0:T(8,128)} fusion(bf16[64,512,128]{2,0,1:T(8,128)(2,1)} %fusion.34, bf16[5,64,128,128]{3,2,1,0:T(8,128)(2,1)} %get-tuple-element.147, s32[]{:T(128)} %get-tuple-element.136), kind=kOutput, calls=%fused_computation.4.clone.1 | convolution fusion | flops 1073741824 | bytes 27263488 | tf_op jit(solution)/shard_map/while/body/eval_jaxpr/jpc,jcd->jpd/dot_general | solution.py:31
  119.5 23.2 %select_add_fusion.2 = f32[32,512,128]{2,0,1:T(8,128)} fusion(f32[32,512,128]{2,0,1:T(8,128)} %get-tuple-element.137, pred[]{:T(512)S(6)} %compare.3, f32[64,512,128]{2,1,0:T(8,128)} %fusion.35, s32[64]{0:T(128)S(1)} %get-tuple-element.128), kind=kOutput, calls=%fused_computation.5.clone.1 | convolution fusion | flops 1614809088 | bytes 33554688 | tf_op jit(solution)/shard_map/while/body/eval_jaxpr/jv,jpd->vpd/dot_general | solution.py:32
  142.7 7.8 %fusion.34 = bf16[64,512,128]{2,0,1:T(8,128)(2,1)} fusion(bf16[512,32,128]{2,1,0:T(8,128)(2,1)} %get-tuple-element.146, s32[64]{0:T(128)S(1)} %get-tuple-element.127), kind=kOutput, calls=%fused_computation.12.clone.1 | convolution fusion | flops 268437504 | bytes 12583168 | tf_op jit(solution)/shard_map/while/body/eval_jaxpr/jt,ptc->jpc/dot_general | solution.py:28
  150.5 18.1 %fusion.35 = f32[64,512,128]{2,1,0:T(8,128)} fusion(bf16[64,512,128]{2,0,1:T(8,128)(2,1)} %fusion.34, bf16[5,64,128,128]{3,2,1,0:T(8,128)(2,1)} %get-tuple-element.147, s32[]{:T(128)} %get-tuple-element.136), kind=kOutput, calls=%fused_computation.4.clone.1 | convolution fusion | flops 1073741824 | bytes 27263488 | tf_op jit(solution)/shard_map/while/body/eval_jaxpr/jpc,jcd->jpd/dot_general | solution.py:31
  168.6 24.4 %select_add_fusion.2 = f32[32,512,128]{2,0,1:T(8,128)} fusion(f32[32,512,128]{2,0,1:T(8,128)} %get-tuple-element.137, pred[]{:T(512)S(6)} %compare.3, f32[64,512,128]{2,1,0:T(8,128)} %fusion.35, s32[64]{0:T(128)S(1)} %get-tuple-element.128), kind=kOutput, calls=%fused_computation.5.clone.1 | convolution fusion | flops 1614809088 | bytes 33554688 | tf_op jit(solution)/shard_map/while/body/eval_jaxpr/jv,jpd->vpd/dot_general | solution.py:32
  193.0 7.8 %fusion.34 = bf16[64,512,128]{2,0,1:T(8,128)(2,1)} fusion(bf16[512,32,128]{2,1,0:T(8,128)(2,1)} %get-tuple-element.146, s32[64]{0:T(128)S(1)} %get-tuple-element.127), kind=kOutput, calls=%fused_computation.12.clone.1 | convolution fusion | flops 268437504 | bytes 12583168 | tf_op jit(solution)/shard_map/while/body/eval_jaxpr/jt,ptc->jpc/dot_general | solution.py:28
  200.8 18.1 %fusion.35 = f32[64,512,128]{2,1,0:T(8,128)} fusion(bf16[64,512,128]{2,0,1:T(8,128)(2,1)} %fusion.34, bf16[5,64,128,128]{3,2,1,0:T(8,128)(2,1)} %get-tuple-element.147, s32[]{:T(128)} %get-tuple-element.136), kind=kOutput, calls=%fused_computation.4.clone.1 | convolution fusion | flops 1073741824 | bytes 27263488 | tf_op jit(solution)/shard_map/while/body/eval_jaxpr/jpc,jcd->jpd/dot_general | solution.py:31
  218.9 24.4 %select_add_fusion.2 = f32[32,512,128]{2,0,1:T(8,128)} fusion(f32[32,512,128]{2,0,1:T(8,128)} %get-tuple-element.137, pred[]{:T(512)S(6)} %compare.3, f32[64,512,128]{2,1,0:T(8,128)} %fusion.35, s32[64]{0:T(128)S(1)} %get-tuple-element.128), kind=kOutput, calls=%fused_computation.5.clone.1 | convolution fusion | flops 1614809088 | bytes 33554688 | tf_op jit(solution)/shard_map/while/body/eval_jaxpr/jv,jpd->vpd/dot_general | solution.py:32
  243.3 7.8 %fusion.34 = bf16[64,512,128]{2,0,1:T(8,128)(2,1)} fusion(bf16[512,32,128]{2,1,0:T(8,128)(2,1)} %get-tuple-element.146, s32[64]{0:T(128)S(1)} %get-tuple-element.127), kind=kOutput, calls=%fused_computation.12.clone.1 | convolution fusion | flops 268437504 | bytes 12583168 | tf_op jit(solution)/shard_map/while/body/eval_jaxpr/jt,ptc->jpc/dot_general | solution.py:28
  251.1 18.1 %fusion.35 = f32[64,512,128]{2,1,0:T(8,128)} fusion(bf16[64,512,128]{2,0,1:T(8,128)(2,1)} %fusion.34, bf16[5,64,128,128]{3,2,1,0:T(8,128)(2,1)} %get-tuple-element.147, s32[]{:T(128)} %get-tuple-element.136), kind=kOutput, calls=%fused_computation.4.clone.1 | convolution fusion | flops 1073741824 | bytes 27263488 | tf_op jit(solution)/shard_map/while/body/eval_jaxpr/jpc,jcd->jpd/dot_general | solution.py:31
  269.2 24.4 %select_add_fusion.2 = f32[32,512,128]{2,0,1:T(8,128)} fusion(f32[32,512,128]{2,0,1:T(8,128)} %get-tuple-element.137, pred[]{:T(512)S(6)} %compare.3, f32[64,512,128]{2,1,0:T(8,128)} %fusion.35, s32[64]{0:T(128)S(1)} %get-tuple-element.128), kind=kOutput, calls=%fused_computation.5.clone.1 | convolution fusion | flops 1614809088 | bytes 33554688 | tf_op jit(solution)/shard_map/while/body/eval_jaxpr/jv,jpd->vpd/dot_general | solution.py:32
  293.6 7.8 %fusion.34 = bf16[64,512,128]{2,0,1:T(8,128)(2,1)} fusion(bf16[512,32,128]{2,1,0:T(8,128)(2,1)} %get-tuple-element.146, s32[64]{0:T(128)S(1)} %get-tuple-element.127), kind=kOutput, calls=%fused_computation.12.clone.1 | convolution fusion | flops 268437504 | bytes 12583168 | tf_op jit(solution)/shard_map/while/body/eval_jaxpr/jt,ptc->jpc/dot_general | solution.py:28
  301.4 18.1 %fusion.35 = f32[64,512,128]{2,1,0:T(8,128)} fusion(bf16[64,512,128]{2,0,1:T(8,128)(2,1)} %fusion.34, bf16[5,64,128,128]{3,2,1,0:T(8,128)(2,1)} %get-tuple-element.147, s32[]{:T(128)} %get-tuple-element.136), kind=kOutput, calls=%fused_computation.4.clone.1 | convolution fusion | flops 1073741824 | bytes 27263488 | tf_op jit(solution)/shard_map/while/body/eval_jaxpr/jpc,jcd->jpd/dot_general | solution.py:31
  319.5 24.4 %select_add_fusion.2 = f32[32,512,128]{2,0,1:T(8,128)} fusion(f32[32,512,128]{2,0,1:T(8,128)} %get-tuple-element.137, pred[]{:T(512)S(6)} %compare.3, f32[64,512,128]{2,1,0:T(8,128)} %fusion.35, s32[64]{0:T(128)S(1)} %get-tuple-element.128), kind=kOutput, calls=%fused_computation.5.clone.1 | convolution fusion | flops 1614809088 | bytes 33554688 | tf_op jit(solution)/shard_map/while/body/eval_jaxpr/jv,jpd->vpd/dot_general | solution.py:32
  343.9 0.0 copy-start.1
  343.9 0.0 all-reduce.2.cloned.1.call-update
  343.9 0.0 all-gather.5.cloned.1.call-start
  344.0 0.5 all-gather.5.cloned.1.call-update
  344.5 0.0 copy-done.1
  344.6 0.1 broadcast_bitcast_fusion
  344.6 268.0 %all-reduce.2.cloned.1.call-done = f32[32,512,128]{2,0,1:T(8,128)} async-done(((f32[32,512,128]{2,0,1:T(8,128)}), f32[32,512,128]{2,0,1:T(8,128)}) %all-reduce.2.cloned.1.call-update) | async-done | bytes 8388624 | tf_op jit(solution)/shard_map/psum | solution.py:39
  612.7 1.8 dynamic-slice_bitcast_fusion
  614.4 1.3 copy.10
  615.8 0.0 all-gather.5.cloned.1.call-done
  615.8 0.0 copy-done
  615.8 3.1 fusion.18
  618.9 1.3 copy.11
  (12 shorter events, 0.1 us)
Async XLA Ops:
  7.4 608.4 %copy-start = (bf16[512,2048]{1,0:T(8,128)(2,1)S(1)}, bf16[512,2048]{1,0:T(8,128)(2,1)}, u32[]{:S(2)}) copy-start(bf16[512,2048]{1,0:T(8,128)(2,1)} %param.12) | copy-start | bytes 6291460
  7.4 80.7 %all-gather.3.cloned.1.call-start = ((), (), s32[]{:S(2)}) async-start(), calls=%async_computation | async-start | bytes 4718592 | tf_op jit(solution)/shard_map/all_gather | solution.py:15
  10.2 602.5 %all-reduce.2.cloned.1.call-start = ((), (), s32[]{:S(2)}) async-start(), calls=%async_computation.1 | async-start | bytes 16777216 | tf_op jit(solution)/shard_map/psum | solution.py:39
  343.9 0.7 copy-start.1
  343.9 271.8 %all-gather.5.cloned.1.call-start = ((), (), s32[]{:S(2)}) async-start(), calls=%async_computation.2 | async-start | bytes 2621440 | tf_op jit(solution)/shard_map/all_gather | solution.py:44
Sparse Core Ops, SparseCore 0:
  10.3 77.7 all-gather.2
  344.1 268.5 all-reduce.1
Sparse Core Ops, SparseCore 1:
  346.0 20.6 all-gather.4
where the time goes:
time: 628 us
  waiting for transfers between devices  346 us (55%)
  matrix products  253 us (40%)
  between operations  14.9 us (2%)
  local copies, waits for them, and re-layouts  11 us (2%)
    psum x1, waiting for transfers between devices, local(): summed = lax.psum(partial_value, 'ints')  268 us
    dot_general x5, matrix products, ladder_step(): jnp.einsum('jv,jpd->vpd', target_table, product, precision=lax.Precision....  121 us
    dot_general x5, matrix products, ladder_step(): jnp.einsum('jpc,jcd->jpd', picked, blocks, preferred_element_type=jnp.flo...  90.6 us
    all_gather x1, waiting for transfers between devices, local(): block_amps = lax.all_gather(amps, 'ints', axis=1, tiled=True)  77 us
    dot_general x5, matrix products, ladder_step(): jnp.einsum('jt,ptc->jpc', source_table, amps_tiled, preferred_element_typ...  39 us
  transfers between devices with their start and end apart: 3, of which 2 were waited for; matrix products, arithmetic and copies ran while one was open for 1% of the time, Pallas kernels for 0%

commit v1 on v0

v1 whole, which is shorter than its diff:
```python
import functools

import jax
import jax.numpy as jnp
from jax import lax
from jax.experimental import pallas as pl
from jax.experimental.pallas import tpu as pltpu
from jax.sharding import PartitionSpec as P

MESH = pl.DeviceIdType.MESH
QROWS = 64
QMAX = 32766.0
GROUP = 4
F32 = jnp.float32


def ring_place(index, n):
    inner = index % 2
    outer = index // 2
    return (1 - inner) * outer + inner * (n - 1 - outer)


def ring_index(place, n):
    place = (place + 2 * n) % n
    half = place // (n // 2)
    return (1 - half) * (2 * place) + half * (2 * (n - 1 - place) + 1)


def enter(n, pairs):
    me = lax.axis_index("ints")
    own_pair = lax.axis_index("pair")
    place = ring_place(me, n)
    nexts = (ring_index(place + 1, n), ring_index(place + n - 1, n))
    barrier = pltpu.get_barrier_semaphore()
    for other in nexts:
        pl.semaphore_signal(barrier, inc=1, device_id=(own_pair, other), device_id_type=MESH)
    for step in range(1, pairs):
        peer = (own_pair + step) % pairs
        pl.semaphore_signal(barrier, inc=1, device_id=(peer, me), device_id_type=MESH)
    pl.semaphore_wait(barrier, 2 + max(pairs - 1, 0))
    return me, own_pair, place, nexts


def gather_kernel(n, pairs, tiles, live_ref, t2_ref, w_ref, all_ref, cycle_ref, own, blocks,
                  send_sem, recv_sem, psend_sem, precv_sem, local_sem):
    rows = t2_ref.shape[0]
    width = t2_ref.shape[1] // tiles
    me, own_pair, place, nexts = enter(n, pairs)
    for t in range(tiles):
        keep = live_ref[0, t].astype(F32)
        own[t] = (t2_ref[:, t * width:(t + 1) * width].astype(F32) * keep).astype(own.dtype)

    def copy_of(step, t):
        way = t * 2 // tiles
        sign = 1 - 2 * way
        slot = ring_index(place + n - sign * step, n) * tiles + t
        return pltpu.make_async_remote_copy(
            src_ref=own.at[t] if step == 0 else all_ref.at[slot],
            dst_ref=all_ref.at[slot],
            send_sem=send_sem.at[t, step],
            recv_sem=recv_sem.at[t, step],
            device_id=(own_pair, nexts[way]),
            device_id_type=MESH,
        )

    half = tiles // 2
    order = [t for c in range(half) for t in (c, half + c)]
    flying = {}
    for t in order:
        flying[t, 0] = copy_of(0, t)
        flying[t, 0].start()
    others = []
    for step in range(1, pairs):
        peer = (own_pair + step) % pairs
        c = pltpu.make_async_remote_copy(
            src_ref=own,
            dst_ref=blocks.at[step],
            send_sem=psend_sem.at[step],
            recv_sem=precv_sem.at[step],
            device_id=(peer, me),
            device_id_type=MESH,
        )
        c.start()
        others.append(c)
    mine = pltpu.make_async_copy(own, all_ref.at[pl.ds(me * tiles, tiles)], local_sem)
    mine.start()

    def add_block(step):
        source = (own_pair + pairs - step) % pairs
        left = w_ref[:, pl.ds(pl.multiple_of(source * rows, 128), rows)]
        for t in range(tiles):
            right = own[t] if step == 0 else blocks[step, t]
            part = jnp.dot(left, right, preferred_element_type=F32)
            if step == 0:
                cycle_ref[t] = part
            else:
                cycle_ref[t] += part

    add_block(0)
    for step in range(1, n - 1):
        for t in order:
            flying[t, step - 1].wait_recv()
            flying[t, step] = copy_of(step, t)
            flying[t, step].start()
        if step == n - 2:
            for k in range(1, pairs):
                others[k - 1].wait_recv()
                add_block(k)
    for t in order:
        flying[t, n - 2].wait_recv()
    for c in flying.values():
        c.wait_send()
    for c in others:
        c.wait_send()
    mine.wait()


def ladder_kernel(table_ref, target_ref, count_ref, amps_ref, ints_ref, out_ref, held, sem):
    count = ints_ref.shape[0]
    load = pltpu.make_async_copy(ints_ref, held.at[pl.ds(0, count)], sem)
    load.start()
    held[count] = jnp.zeros(held.shape[1:], held.dtype)
    load.wait()

    def step(s, last):
        target = target_ref[s]
        first = target != last
        picks = [table_ref[0, s * GROUP + g] for g in range(GROUP)]
        sources = [table_ref[1, s * GROUP + g] for g in range(GROUP)]
        left = jnp.concatenate([amps_ref[u] for u in sources], axis=1)
        right = jnp.concatenate([held[j] for j in picks], axis=0)
        part = jnp.dot(left, right, preferred_element_type=F32)

        @pl.when(first)
        def _():
            out_ref[target] = part

        @pl.when(jnp.logical_not(first))
        def _():
            out_ref[target] += part

        return target

    lax.fori_loop(0, count_ref[0], step, jnp.int32(-1))


def reduce_kernel(n, pairs, tiles, keep_ref, cycle_ref, part_ref, out_ref, held, sent, sent_scale,
                  got, got_scale, load_sem, send_sem, recv_sem, ssend_sem, srecv_sem):
    rows = cycle_ref.shape[1]
    width = cycle_ref.shape[2]
    chunks = rows // QROWS
    half = tiles // 2
    order = [t for c in range(half) for t in (c, half + c)]
    own_pair = lax.axis_index("pair")
    place = ring_place(lax.axis_index("ints"), n)

    def slot_of(step, t):
        sign = 1 - 2 * (t * 2 // tiles)
        return ring_index(place + 2 * n - sign * (step + 1), n) * tiles + t

    loads = {}
    for step in range(n):
        for t in order:
            loads[t, step] = pltpu.make_async_copy(
                part_ref.at[slot_of(step, t)], held.at[t, step], load_sem.at[t, step]
            )
            loads[t, step].start()
    me, own_pair, place, nexts = enter(n, 1)

    def total(step, t, k):
        at = pl.ds(pl.multiple_of(k * QROWS, QROWS), QROWS)
        value = held[t, step, at, :]
        if step > 0:
            scale = got_scale[t, step - 1, pl.ds(k, 1), :]
            value = value + got[t, step - 1, at, :].astype(jnp.int32).astype(F32) * scale
        return at, value

    def pack(step, t):
        def body(k, carry):
            at, value = total(step, t, k)
            top = jnp.maximum(jnp.max(jnp.abs(value), axis=0, keepdims=True), 1e-30)
            sent_scale[t, step, pl.ds(k, 1), :] = top * (1.0 / QMAX)
            scaled = jnp.round(value * (QMAX / top))
            sent[t, step, at, :] = scaled.astype(jnp.int32).astype(jnp.int16)
            return carry

        lax.fori_loop(0, chunks, body, 0)

    def copies(step, t):
        way = t * 2 // tiles
        where = (own_pair, nexts[way])
        return [
            pltpu.make_async_remote_copy(
                src_ref=a.at[t, step], dst_ref=b.at[t, step], send_sem=c.at[t, step],
                recv_sem=d.at[t, step], device_id=where, device_id_type=MESH,
            )
            for a, b, c, d in (
                (sent, got, send_sem, recv_sem),
                (sent_scale, got_scale, ssend_sem, srecv_sem),
            )
        ]

    flying = {}
    for step in range(n - 1):
        for t in order:
            loads[t, step].wait()
            if step > 0:
                for c in flying[t, step - 1]:
                    c.wait_recv()
            pack(step, t)
            flying[t, step] = copies(step, t)
            for c in flying[t, step]:
                c.start()
    for t in order:
        loads[t, n - 1].wait()
        for c in flying[t, n - 2]:
            c.wait_recv()
        keep = keep_ref[0, t].astype(F32)

        def body(k, carry):
            at, value = total(n - 1, t, k)
            out_ref[at, t * width:(t + 1) * width] = (value + cycle_ref[t, at, :]) * keep
            return carry

        lax.fori_loop(0, chunks, body, 0)
    for pair_of in flying.values():
        for c in pair_of:
            c.wait_send()


def tables(int_tiles, tiles_all):
    count = int_tiles.shape[0]
    slots = (count + GROUP * tiles_all) // GROUP
    u, v = int_tiles[:, 0], int_tiles[:, 1]
    ids = jnp.arange(count, dtype=jnp.int32)
    tile_ids = jnp.arange(tiles_all, dtype=jnp.int32)
    rank = jnp.sum((v[:, None] == v[None, :]) & (ids[None, :] < ids[:, None]), axis=1, dtype=jnp.int32)
    counts = jnp.sum(v[:, None] == tile_ids[None, :], axis=0, dtype=jnp.int32)
    groups = jnp.maximum((counts + GROUP - 1) // GROUP, 1)
    ends = jnp.sum(jnp.where(tile_ids[:, None] >= tile_ids[None, :], groups[None, :], 0), axis=1)
    base = jnp.sum(jnp.where(tile_ids[None, :] < v[:, None], groups[None, :], 0), axis=1)
    spot = base * GROUP + rank
    hit = spot[None, :] == jnp.arange(slots * GROUP, dtype=jnp.int32)[:, None]
    picks = count + jnp.sum(jnp.where(hit, ids[None, :] - count, 0), axis=1)
    sources = jnp.sum(jnp.where(hit, u[None, :], 0), axis=1)
    target = jnp.sum(ends[None, :] <= jnp.arange(slots, dtype=jnp.int32)[:, None], axis=1, dtype=jnp.int32)
    return jnp.stack([picks, sources]), target, ends[-1:]


def vmem():
    return pl.BlockSpec(memory_space=pltpu.VMEM)


def smem():
    return pl.BlockSpec(memory_space=pltpu.SMEM)


def anywhere():
    return pl.BlockSpec(memory_space=pl.ANY)


def local(n, pairs, t2, t2_live, int_tiles, integrals, cycle_w, res_live):
    rows = t2.shape[0]
    width = integrals.shape[1]
    tiles = t2.shape[1] // width
    tiles_all = tiles * n
    count = integrals.shape[0]
    dma = pltpu.SemaphoreType.DMA
    amps, cycle = pl.pallas_call(
        functools.partial(gather_kernel, n, pairs, tiles),
        out_shape=(
            jax.ShapeDtypeStruct((tiles_all, rows, width), t2.dtype),
            jax.ShapeDtypeStruct((tiles, rows, width), F32),
        ),
        in_specs=[smem(), vmem(), vmem()],
        out_specs=(anywhere(), vmem()),
        scratch_shapes=[
            pltpu.VMEM((tiles, rows, width), t2.dtype),
            pltpu.VMEM((pairs, tiles, rows, width), t2.dtype),
            dma((tiles, n)), dma((tiles, n)), dma((pairs,)), dma((pairs,)), dma,
        ],
        compiler_params=pltpu.CompilerParams(
            collective_id=0, has_side_effects=True, vmem_limit_bytes=48 << 20
        ),
        name="gather_amps",
    )(t2_live, t2, cycle_w)

    table, target, steps = tables(int_tiles, tiles_all)
    partial = pl.pallas_call(
        ladder_kernel,
        out_shape=jax.ShapeDtypeStruct((tiles_all, rows, width), F32),
        in_specs=[smem(), smem(), smem(), vmem(), anywhere()],
        out_specs=vmem(),
        scratch_shapes=[pltpu.VMEM((count + 1, width, width), integrals.dtype), dma],
        compiler_params=pltpu.CompilerParams(vmem_limit_bytes=56 << 20),
        name="ladder_partial",
    )(table, target, steps, amps, integrals)

    chunks = rows // QROWS
    return pl.pallas_call(
        functools.partial(reduce_kernel, n, pairs, tiles),
        out_shape=jax.ShapeDtypeStruct((rows, tiles * width), F32),
        in_specs=[smem(), vmem(), anywhere()],
        out_specs=vmem(),
        scratch_shapes=[
            pltpu.VMEM((tiles, n, rows, width), F32),
            pltpu.VMEM((tiles, n - 1, rows, width), jnp.int16),
            pltpu.VMEM((tiles, n - 1, chunks, width), F32),
            pltpu.VMEM((tiles, n - 1, rows, width), jnp.int16),
            pltpu.VMEM((tiles, n - 1, chunks, width), F32),
            dma((tiles, n)), dma((tiles, n)), dma((tiles, n)), dma((tiles, n)), dma((tiles, n)),
        ],
        compiler_params=pltpu.CompilerParams(
            collective_id=1, has_side_effects=True, vmem_limit_bytes=56 << 20
        ),
        name="reduce_partial",
    )(res_live, cycle, partial)


def solution(mesh):
    n = mesh.shape["ints"]
    pairs = mesh.shape["pair"]
    placed = (
        P("pair", "ints"),
        P("pair", "ints"),
        P("ints", None),
        P("ints", None, None),
        P("pair", None),
        P("pair", "ints"),
    )
    return jax.shard_map(
        functools.partial(local, n, pairs), mesh=mesh, in_specs=placed,
        out_specs=P("pair", "ints"), check_vma=False
    )
```

time: 628 us -> 145 us (0.23)
  waiting for transfers between devices: 346 us -> 0 us
  matrix products: 253 us -> 0 us
  Pallas kernels: 0 us -> 135 us
  between operations: 14.9 us -> 0.06 us
    psum x1 -> x0, waiting for transfers between devices: 268 us -> none  [local(): summed = lax.psum(partial_value, 'ints')]
    dot_general x16 -> x0, matrix products: 253 us -> none  [the longest x5 121 us: ladder_step(): jnp.einsum('jv,jpd->vpd', target_table, product, precision=lax.Precision....]
    pallas_call x0 -> x3, Pallas kernels: none -> 135 us  [the longest x1 49 us: local(): pl.pallas_call(functools.partial(reduce_kernel, n, pairs, tiles), out_sha...]
    all_gather x2 -> x0, waiting for transfers between devices: 77 us -> none  [the longest x1 77 us: local(): block_amps = lax.all_gather(amps, 'ints', axis=1, tiled=True)]
  transfers between devices with their start and end apart: 3 -> 0, of which waited for: 2 -> 0; matrix products, arithmetic and copies ran while one was open for 1% -> 0% of each run, Pallas kernels for 0% -> 0%
where the time goes in v1:
time: 145 us
  Pallas kernels  135 us (93%)
  local copies, waits for them, and re-layouts  7.95 us (5%)
  other arithmetic  2.04 us (1%)
    pallas_call x1, Pallas kernels, local(): pl.pallas_call(functools.partial(reduce_kernel, n, pairs, tiles), out_sha...  49 us
    pallas_call x1, Pallas kernels, local(): pl.pallas_call(functools.partial(gather_kernel, n, pairs, tiles), out_sha...  46.7 us
    pallas_call x1, Pallas kernels, local(): pl.pallas_call(ladder_kernel, out_shape=jax.ShapeDtypeStruct((tiles_all,...  39.4 us
    unnamed x9, local copies, waits for them, and re-layouts  6.51 us

profile of v1, /device:TPU:0, one launch (start us, length us, event | category | flops | bytes accessed | tf_op | source)
XLA Modules:
  0.0 145.1 jit_solution(5786532879883184428)
XLA Ops:
  0.0 0.8 slice_reduce_fusion.1
  0.8 0.1 convert_reduce_fusion.1
  0.9 0.1 select_reduce_fusion.3
  1.0 0.7 slice.11.count_ref
  1.7 0.7 convert_reduce_fusion.2.target_ref
  2.3 0.1 select_reduce_fusion.2
  2.4 0.2 convert_reduce_fusion
  2.7 0.2 select_reduce_fusion.1
  2.9 0.6 pad_add_fusion.table_ref
  3.5 0.0 copy-start
  3.5 1.6 %copy-done = bf16[512,2048]{1,0:T(8,128)(2,1)S(1)} copy-done((bf16[512,2048]{1,0:T(8,128)(2,1)S(1)}, bf16[512,2048]{1,0:T(8,128)(2,1)}, u32[]{:S(2)}) %copy-start) | copy-done | bytes 2097176
  5.1 0.0 copy-start.2
  5.1 1.0 copy-done.2
  6.1 0.0 copy-start.3
  6.1 0.7 copy-done.3
  6.8 46.7 %gather_amps.1 = (bf16[32,512,128]{2,1,0:T(8,128)(2,1)}, f32[4,512,128]{2,1,0:T(8,128)S(1)}) custom-call(s32[1,4]{1,0:T(1,128)S(1)} %copy-done.3, bf16[512,512]{1,0:T(8,128)(2,1)S(1)} %copy-done.2, bf16[512,2048]{1,0:T(8,128)(2,1)S(1)} %copy-done), custom_call_target="tpu_custom_call" | custom-call | tf_op jit(solution)/shard_map/gather_amps/pallas_call | solution.py:269
  53.5 0.0 copy-start.1
  53.5 1.0 copy-done.1
  54.4 39.4 %ladder_partial.1.part_ref = f32[32,512,128]{2,1,0:T(8,128)} custom-call(s32[2,448]{1,0:T(2,128)} %pad_add_fusion.table_ref, s32[112]{0:T(128)} %convert_reduce_fusion.2.target_ref, s32[1]{0:T(128)} %slice.11.count_ref, bf16[32,512,128]{2,1,0:T(8,128)(2,1)} %get-tuple-element.8.amps_ref, bf16[320,128,128]{2,1,0:T(8,128)(2,1)} %ints_ref.1), custom_call_target="tpu_custom_call" | custom-call | tf_op jit(solution)/shard_map/ladder_partial/pallas_call | solution.py:289
  93.8 49.0 %reduce_partial.1 = f32[512,512]{1,0:T(8,128)} custom-call(s32[1,4]{1,0:T(1,128)} %keep_ref.1, f32[4,512,128]{2,1,0:T(8,128)} %copy-done.1, f32[32,512,128]{2,1,0:T(8,128)} %ladder_partial.1.part_ref), custom_call_target="tpu_custom_call" | custom-call | tf_op jit(solution)/shard_map/reduce_partial/pallas_call | solution.py:300
  142.8 2.3 %copy.8 = f32[512,512]{1,0:T(8,128)} copy(f32[512,512]{1,0:T(8,128)} %reduce_partial.1) | data formatting | bytes 2097152
  (3 shorter events, 0.0 us)
Async XLA Ops:
  3.5 1.6 %copy-start = (bf16[512,2048]{1,0:T(8,128)(2,1)S(1)}, bf16[512,2048]{1,0:T(8,128)(2,1)}, u32[]{:S(2)}) copy-start(bf16[512,2048]{1,0:T(8,128)(2,1)} %w_ref.1) | copy-start | bytes 6291460
  5.1 1.0 copy-start.2
  6.1 0.7 copy-start.3
  53.5 1.0 copy-start.1

commit v2 on v1

--- a/solution.py
+++ b/solution.py
@@ -11,6 +11,8 @@
 QROWS = 64
 QMAX = 32766.0
 GROUP = 4
+UNROLL = 4
+PHASE = 4
 F32 = jnp.float32
 
 
@@ -41,11 +43,16 @@
     return me, own_pair, place, nexts
 
 
-def gather_kernel(n, pairs, tiles, live_ref, t2_ref, w_ref, all_ref, cycle_ref, own, blocks,
-                  send_sem, recv_sem, psend_sem, precv_sem, local_sem):
+def gather_kernel(n, pairs, tiles, live_ref, t2_hbm, w_hbm, all_ref, cycle_hbm, own, blocks, t2_ref,
+                  w_ref, cycle_ref, send_sem, recv_sem, psend_sem, precv_sem, local_sem):
     rows = t2_ref.shape[0]
     width = t2_ref.shape[1] // tiles
+    t2_load = pltpu.make_async_copy(t2_hbm, t2_ref, local_sem.at[1])
+    t2_load.start()
+    w_load = pltpu.make_async_copy(w_hbm, w_ref, local_sem.at[2])
+    w_load.start()
     me, own_pair, place, nexts = enter(n, pairs)
+    t2_load.wait()
     for t in range(tiles):
         keep = live_ref[0, t].astype(F32)
         own[t] = (t2_ref[:, t * width:(t + 1) * width].astype(F32) * keep).astype(own.dtype)
@@ -82,7 +89,7 @@
         )
         c.start()
         others.append(c)
-    mine = pltpu.make_async_copy(own, all_ref.at[pl.ds(me * tiles, tiles)], local_sem)
+    mine = pltpu.make_async_copy(own, all_ref.at[pl.ds(me * tiles, tiles)], local_sem.at[0])
     mine.start()
 
     def add_block(step):
@@ -96,6 +103,7 @@
             else:
                 cycle_ref[t] += part
 
+    w_load.wait()
     add_block(0)
     for step in range(1, n - 1):
         for t in order:
@@ -106,6 +114,8 @@
             for k in range(1, pairs):
                 others[k - 1].wait_recv()
                 add_block(k)
+            cycle_out = pltpu.make_async_copy(cycle_ref, cycle_hbm, local_sem.at[1])
+            cycle_out.start()
     for t in order:
         flying[t, n - 2].wait_recv()
     for c in flying.values():
@@ -113,39 +123,62 @@
     for c in others:
         c.wait_send()
     mine.wait()
-
-
-def ladder_kernel(table_ref, target_ref, count_ref, amps_ref, ints_ref, out_ref, held, sem):
-    count = ints_ref.shape[0]
-    load = pltpu.make_async_copy(ints_ref, held.at[pl.ds(0, count)], sem)
-    load.start()
+    cycle_out.wait()
+
+
+def ladder_kernel(table_ref, target_ref, ends_ref, amps_hbm, ints_hbm, out_hbm, amps, held, acc,
+                  sem, out_sem):
+    count = ints_hbm.shape[0]
+    tiles_all = acc.shape[0]
+    loads = (
+        pltpu.make_async_copy(amps_hbm, amps, sem.at[0]),
+        pltpu.make_async_copy(ints_hbm, held.at[pl.ds(0, count)], sem.at[1]),
+    )
+    for c in loads:
+        c.start()
     held[count] = jnp.zeros(held.shape[1:], held.dtype)
-    load.wait()
-
-    def step(s, last):
-        target = target_ref[s]
-        first = target != last
-        picks = [table_ref[0, s * GROUP + g] for g in range(GROUP)]
-        sources = [table_ref[1, s * GROUP + g] for g in range(GROUP)]
-        left = jnp.concatenate([amps_ref[u] for u in sources], axis=1)
-        right = jnp.concatenate([held[j] for j in picks], axis=0)
-        part = jnp.dot(left, right, preferred_element_type=F32)
-
-        @pl.when(first)
-        def _():
-            out_ref[target] = part
-
-        @pl.when(jnp.logical_not(first))
-        def _():
-            out_ref[target] += part
-
-        return target
-
-    lax.fori_loop(0, count_ref[0], step, jnp.int32(-1))
-
-
-def reduce_kernel(n, pairs, tiles, keep_ref, cycle_ref, part_ref, out_ref, held, sent, sent_scale,
-                  got, got_scale, load_sem, send_sem, recv_sem, ssend_sem, srecv_sem):
+
+    def clear(t, carry):
+        acc[t] = jnp.zeros(acc.shape[1:], acc.dtype)
+        return carry
+
+    lax.fori_loop(0, tiles_all, clear, 0)
+    for c in loads:
+        c.wait()
+
+    def step(i, carry):
+        for k in range(UNROLL):
+            s = i * UNROLL + k
+            left = jnp.concatenate(
+                [amps[table_ref[1, s * GROUP + g]] for g in range(GROUP)], axis=1
+            )
+            right = jnp.concatenate(
+                [held[table_ref[0, s * GROUP + g]] for g in range(GROUP)], axis=0
+            )
+            acc[target_ref[s]] += jnp.dot(left, right, preferred_element_type=F32)
+        return carry
+
+    def store_of(phase):
+        at = pl.ds(pl.multiple_of(phase * PHASE, PHASE), PHASE)
+        return pltpu.make_async_copy(acc.at[at], out_hbm.at[at], out_sem.at[phase])
+
+    def run_phase(phase, low):
+        high = (ends_ref[(phase + 1) * PHASE - 1] + UNROLL - 1) // UNROLL
+        lax.fori_loop(low, high, step, 0)
+        store_of(phase).start()
+        return high
+
+    def finish(phase, carry):
+        store_of(phase).wait()
+        return carry
+
+    phases = tiles_all // PHASE
+    lax.fori_loop(0, phases, run_phase, jnp.int32(0))
+    lax.fori_loop(0, phases, finish, 0)
+
+
+def reduce_kernel(n, pairs, tiles, keep_ref, cycle_hbm, part_ref, out_ref, cycle_ref, held, sent, sent_scale,
+                  got, got_scale, cycle_sem, load_sem, send_sem, recv_sem, ssend_sem, srecv_sem):
     rows = cycle_ref.shape[1]
     width = cycle_ref.shape[2]
     chunks = rows // QROWS
@@ -165,6 +198,8 @@
                 part_ref.at[slot_of(step, t)], held.at[t, step], load_sem.at[t, step]
             )
             loads[t, step].start()
+    cycle_load = pltpu.make_async_copy(cycle_hbm, cycle_ref, cycle_sem)
+    cycle_load.start()
     me, own_pair, place, nexts = enter(n, 1)
 
     def total(step, t, k):
@@ -211,6 +246,7 @@
             flying[t, step] = copies(step, t)
             for c in flying[t, step]:
                 c.start()
+    cycle_load.wait()
     for t in order:
         loads[t, n - 1].wait()
         for c in flying[t, n - 2]:
@@ -230,13 +266,14 @@
 
 def tables(int_tiles, tiles_all):
     count = int_tiles.shape[0]
-    slots = (count + GROUP * tiles_all) // GROUP
+    slots = (count + (GROUP - 1) * tiles_all) // GROUP
+    slots = (slots + UNROLL - 1) // UNROLL * UNROLL
     u, v = int_tiles[:, 0], int_tiles[:, 1]
     ids = jnp.arange(count, dtype=jnp.int32)
     tile_ids = jnp.arange(tiles_all, dtype=jnp.int32)
     rank = jnp.sum((v[:, None] == v[None, :]) & (ids[None, :] < ids[:, None]), axis=1, dtype=jnp.int32)
     counts = jnp.sum(v[:, None] == tile_ids[None, :], axis=0, dtype=jnp.int32)
-    groups = jnp.maximum((counts + GROUP - 1) // GROUP, 1)
+    groups = (counts + GROUP - 1) // GROUP
     ends = jnp.sum(jnp.where(tile_ids[:, None] >= tile_ids[None, :], groups[None, :], 0), axis=1)
     base = jnp.sum(jnp.where(tile_ids[None, :] < v[:, None], groups[None, :], 0), axis=1)
     spot = base * GROUP + rank
@@ -244,7 +281,7 @@
     picks = count + jnp.sum(jnp.where(hit, ids[None, :] - count, 0), axis=1)
     sources = jnp.sum(jnp.where(hit, u[None, :], 0), axis=1)
     target = jnp.sum(ends[None, :] <= jnp.arange(slots, dtype=jnp.int32)[:, None], axis=1, dtype=jnp.int32)
-    return jnp.stack([picks, sources]), target, ends[-1:]
+    return jnp.stack([picks, sources]), jnp.minimum(target, tiles_all - 1), ends
 
 
 def vmem():
@@ -272,12 +309,15 @@
             jax.ShapeDtypeStruct((tiles_all, rows, width), t2.dtype),
             jax.ShapeDtypeStruct((tiles, rows, width), F32),
         ),
-        in_specs=[smem(), vmem(), vmem()],
-        out_specs=(anywhere(), vmem()),
+        in_specs=[smem(), anywhere(), anywhere()],
+        out_specs=(anywhere(), anywhere()),
         scratch_shapes=[
             pltpu.VMEM((tiles, rows, width), t2.dtype),
             pltpu.VMEM((pairs, tiles, rows, width), t2.dtype),
-            dma((tiles, n)), dma((tiles, n)), dma((pairs,)), dma((pairs,)), dma,
+            pltpu.VMEM(t2.shape, t2.dtype),
+            pltpu.VMEM(cycle_w.shape, cycle_w.dtype),
+            pltpu.VMEM((tiles, rows, width), F32),
+            dma((tiles, n)), dma((tiles, n)), dma((pairs,)), dma((pairs,)), dma((3,)),
         ],
         compiler_params=pltpu.CompilerParams(
             collective_id=0, has_side_effects=True, vmem_limit_bytes=48 << 20
@@ -289,9 +329,14 @@
     partial = pl.pallas_call(
         ladder_kernel,
         out_shape=jax.ShapeDtypeStruct((tiles_all, rows, width), F32),
-        in_specs=[smem(), smem(), smem(), vmem(), anywhere()],
-        out_specs=vmem(),
-        scratch_shapes=[pltpu.VMEM((count + 1, width, width), integrals.dtype), dma],
+        in_specs=[smem(), smem(), smem(), anywhere(), anywhere()],
+        out_specs=anywhere(),
+        scratch_shapes=[
+            pltpu.VMEM((tiles_all, rows, width), t2.dtype),
+            pltpu.VMEM((count + 1, width, width), integrals.dtype),
+            pltpu.VMEM((tiles_all, rows, width), F32),
+            dma((2,)), dma((tiles_all // PHASE,)),
+        ],
         compiler_params=pltpu.CompilerParams(vmem_limit_bytes=56 << 20),
         name="ladder_partial",
     )(table, target, steps, amps, integrals)
@@ -300,15 +345,16 @@
     return pl.pallas_call(
         functools.partial(reduce_kernel, n, pairs, tiles),
         out_shape=jax.ShapeDtypeStruct((rows, tiles * width), F32),
-        in_specs=[smem(), vmem(), anywhere()],
+        in_specs=[smem(), anywhere(), anywhere()],
         out_specs=vmem(),
         scratch_shapes=[
+            pltpu.VMEM((tiles, rows, width), F32),
             pltpu.VMEM((tiles, n, rows, width), F32),
             pltpu.VMEM((tiles, n - 1, rows, width), jnp.int16),
             pltpu.VMEM((tiles, n - 1, chunks, width), F32),
             pltpu.VMEM((tiles, n - 1, rows, width), jnp.int16),
             pltpu.VMEM((tiles, n - 1, chunks, width), F32),
-            dma((tiles, n)), dma((tiles, n)), dma((tiles, n)), dma((tiles, n)), dma((tiles, n)),
+            dma, dma((tiles, n)), dma((tiles, n)), dma((tiles, n)), dma((tiles, n)), dma((tiles, n)),
         ],
         compiler_params=pltpu.CompilerParams(
             collective_id=1, has_side_effects=True, vmem_limit_bytes=56 << 20

time: 145 us -> 129 us (0.89)
  Pallas kernels: 135 us -> 119 us
    pallas_call x1, Pallas kernels: 39.4 us -> 24.6 us  [local(): pl.pallas_call(ladder_kernel, out_shape=jax.ShapeDtypeStruct((tiles_all,...]
    unnamed x9 -> x11, local copies, waits for them, and re-layouts: 6.51 us -> 6.52 us
where the time goes in v2:
time: 129 us
  Pallas kernels  119 us (92%)
  local copies, waits for them, and re-layouts  7.3 us (6%)
  other arithmetic  2.13 us (2%)
    pallas_call x1, Pallas kernels, local(): pl.pallas_call(functools.partial(reduce_kernel, n, pairs, tiles), out_sha...  47.9 us
    pallas_call x1, Pallas kernels, local(): pl.pallas_call(functools.partial(gather_kernel, n, pairs, tiles), out_sha...  46.9 us
    pallas_call x1, Pallas kernels, local(): pl.pallas_call(ladder_kernel, out_shape=jax.ShapeDtypeStruct((tiles_all,...  24.6 us
    unnamed x11, local copies, waits for them, and re-layouts  6.52 us

profile of v2, /device:TPU:0, one launch (start us, length us, event | category | flops | bytes accessed | tf_op | source)
XLA Modules:
  0.0 128.8 jit_solution(7121351637360934124)
XLA Ops:
  0.0 0.8 slice_reduce_fusion.1
  0.8 0.1 convert_reduce_fusion.1
  0.9 0.1 select_reduce_fusion.3.ends_ref
  1.0 0.0 copy-start.4
  1.0 0.1 convert_reduce_fusion.2
  1.1 0.6 broadcast_minimum_fusion.target_ref
  1.7 0.1 select_reduce_fusion.2
  1.8 0.2 convert_reduce_fusion
  2.0 0.3 select_reduce_fusion.1
  2.3 0.6 pad_add_fusion.table_ref
  2.9 0.0 copy-start
  2.9 1.6 %copy-done = bf16[512,2048]{1,0:T(8,128)(2,1)S(1)} copy-done((bf16[512,2048]{1,0:T(8,128)(2,1)S(1)}, bf16[512,2048]{1,0:T(8,128)(2,1)}, u32[]{:S(2)}) %copy-start) | copy-done | bytes 2097176
  4.5 0.0 copy-start.2
  4.5 1.0 copy-done.2
  5.6 0.0 copy-start.3
  5.6 0.7 copy-done.3
  6.2 46.9 %gather_amps.1 = (bf16[32,512,128]{2,1,0:T(8,128)(2,1)}, f32[4,512,128]{2,1,0:T(8,128)S(1)}) custom-call(s32[1,4]{1,0:T(1,128)S(1)} %copy-done.3, bf16[512,512]{1,0:T(8,128)(2,1)S(1)} %copy-done.2, bf16[512,2048]{1,0:T(8,128)(2,1)S(1)} %copy-done), custom_call_target="tpu_custom_call" | custom-call | tf_op jit(solution)/shard_map/gather_amps/pallas_call | solution.py:306
  53.1 0.0 copy-start.1
  53.1 1.0 copy-done.1
  54.1 0.0 copy-done.4
  54.1 24.6 %ladder_partial.1.part_ref = f32[32,512,128]{2,1,0:T(8,128)} custom-call(s32[2,416]{1,0:T(2,128)} %pad_add_fusion.table_ref, s32[104]{0:T(128)} %broadcast_minimum_fusion.target_ref, s32[32]{0:T(128)} %copy-done.4, bf16[32,512,128]{2,1,0:T(8,128)(2,1)} %get-tuple-element.8.amps_hbm, bf16[320,128,128]{2,1,0:T(8,128)(2,1)} %ints_hbm.1), custom_call_target="tpu_custom_call" | custom-call | tf_op jit(solution)/shard_map/ladder_partial/pallas_call | solution.py:329
  78.6 47.9 %reduce_partial.1 = f32[512,512]{1,0:T(8,128)} custom-call(s32[1,4]{1,0:T(1,128)} %keep_ref.1, f32[4,512,128]{2,1,0:T(8,128)} %copy-done.1, f32[32,512,128]{2,1,0:T(8,128)} %ladder_partial.1.part_ref), custom_call_target="tpu_custom_call" | custom-call | tf_op jit(solution)/shard_map/reduce_partial/pallas_call | solution.py:345
  126.5 2.3 %copy.8 = f32[512,512]{1,0:T(8,128)} copy(f32[512,512]{1,0:T(8,128)} %reduce_partial.1) | data formatting | bytes 2097152
  (3 shorter events, 0.0 us)
Async XLA Ops:
  1.0 53.0 %copy-start.4 = (s32[32]{0:T(128)}, s32[32]{0:T(128)S(1)}, u32[]{:S(2)}) copy-start(s32[32]{0:T(128)S(1)} %select_reduce_fusion.3.ends_ref) | copy-start | bytes 388
  2.9 1.6 %copy-start = (bf16[512,2048]{1,0:T(8,128)(2,1)S(1)}, bf16[512,2048]{1,0:T(8,128)(2,1)}, u32[]{:S(2)}) copy-start(bf16[512,2048]{1,0:T(8,128)(2,1)} %w_hbm.1) | copy-start | bytes 6291460
  4.5 1.0 copy-start.2
  5.6 0.7 copy-start.3
  53.1 1.0 copy-start.1

commit v3 on v2

--- a/solution.py
+++ b/solution.py
@@ -51,11 +51,11 @@
     t2_load.start()
     w_load = pltpu.make_async_copy(w_hbm, w_ref, local_sem.at[2])
     w_load.start()
-    me, own_pair, place, nexts = enter(n, pairs)
     t2_load.wait()
     for t in range(tiles):
         keep = live_ref[0, t].astype(F32)
         own[t] = (t2_ref[:, t * width:(t + 1) * width].astype(F32) * keep).astype(own.dtype)
+    me, own_pair, place, nexts = enter(n, pairs)
 
     def copy_of(step, t):
         way = t * 2 // tiles
@@ -126,11 +126,14 @@
     cycle_out.wait()
 
 
-def ladder_kernel(table_ref, target_ref, ends_ref, amps_hbm, ints_hbm, out_hbm, amps, held, acc,
-                  sem, out_sem):
+def ladder_kernel(table_hbm, target_hbm, ends_hbm, amps_hbm, ints_hbm, out_hbm, table_ref,
+                  target_ref, ends_ref, amps, held, acc, sem, out_sem):
     count = ints_hbm.shape[0]
     tiles_all = acc.shape[0]
     loads = (
+        pltpu.make_async_copy(table_hbm, table_ref, sem.at[2]),
+        pltpu.make_async_copy(target_hbm, target_ref, sem.at[3]),
+        pltpu.make_async_copy(ends_hbm, ends_ref, sem.at[4]),
         pltpu.make_async_copy(amps_hbm, amps, sem.at[0]),
         pltpu.make_async_copy(ints_hbm, held.at[pl.ds(0, count)], sem.at[1]),
     )
@@ -200,7 +203,6 @@
             loads[t, step].start()
     cycle_load = pltpu.make_async_copy(cycle_hbm, cycle_ref, cycle_sem)
     cycle_load.start()
-    me, own_pair, place, nexts = enter(n, 1)
 
     def total(step, t, k):
         at = pl.ds(pl.multiple_of(k * QROWS, QROWS), QROWS)
@@ -221,6 +223,11 @@
 
         lax.fori_loop(0, chunks, body, 0)
 
+    for t in order:
+        loads[t, 0].wait()
+        pack(0, t)
+    me, own_pair, place, nexts = enter(n, 1)
+
     def copies(step, t):
         way = t * 2 // tiles
         where = (own_pair, nexts[way])
@@ -238,11 +245,11 @@
     flying = {}
     for step in range(n - 1):
         for t in order:
-            loads[t, step].wait()
             if step > 0:
+                loads[t, step].wait()
                 for c in flying[t, step - 1]:
                     c.wait_recv()
-            pack(step, t)
+                pack(step, t)
             flying[t, step] = copies(step, t)
             for c in flying[t, step]:
                 c.start()
@@ -329,13 +336,16 @@
     partial = pl.pallas_call(
         ladder_kernel,
         out_shape=jax.ShapeDtypeStruct((tiles_all, rows, width), F32),
-        in_specs=[smem(), smem(), smem(), anywhere(), anywhere()],
+        in_specs=[anywhere()] * 5,
         out_specs=anywhere(),
         scratch_shapes=[
+            pltpu.SMEM(table.shape, table.dtype),
+            pltpu.SMEM(target.shape, target.dtype),
+            pltpu.SMEM(steps.shape, steps.dtype),
             pltpu.VMEM((tiles_all, rows, width), t2.dtype),
             pltpu.VMEM((count + 1, width, width), integrals.dtype),
             pltpu.VMEM((tiles_all, rows, width), F32),
-            dma((2,)), dma((tiles_all // PHASE,)),
+            dma((5,)), dma((tiles_all // PHASE,)),
         ],
         compiler_params=pltpu.CompilerParams(vmem_limit_bytes=56 << 20),
         name="ladder_partial",

time: 129 us -> 129 us (level)
    pallas_call x1, Pallas kernels: 47.9 us -> 49.8 us  [local(): pl.pallas_call(functools.partial(reduce_kernel, n, pairs, tiles), out_sha...]
    pallas_call x1, Pallas kernels: 24.6 us -> 23.1 us  [local(): pl.pallas_call(ladder_kernel, out_shape=jax.ShapeDtypeStruct((tiles_all,...]
where the time goes in v3:
time: 129 us
  Pallas kernels  120 us (93%)
  local copies, waits for them, and re-layouts  7.3 us (6%)
  other arithmetic  2.13 us (2%)
    pallas_call x1, Pallas kernels, local(): pl.pallas_call(functools.partial(reduce_kernel, n, pairs, tiles), out_sha...  49.8 us
    pallas_call x1, Pallas kernels, local(): pl.pallas_call(functools.partial(gather_kernel, n, pairs, tiles), out_sha...  46.8 us
    pallas_call x1, Pallas kernels, local(): pl.pallas_call(ladder_kernel, out_shape=jax.ShapeDtypeStruct((tiles_all,...  23.1 us
    unnamed x11, local copies, waits for them, and re-layouts  6.52 us

profile of v3, /device:TPU:0, one launch (start us, length us, event | category | flops | bytes accessed | tf_op | source)
XLA Modules:
  0.0 129.3 jit_solution(7830866842117332703)
XLA Ops:
  0.0 0.8 slice_reduce_fusion.1
  0.8 0.1 convert_reduce_fusion.1
  0.9 0.1 select_reduce_fusion.3.ends_hbm
  1.0 0.0 copy-start.4
  1.0 0.1 convert_reduce_fusion.2
  1.1 0.6 broadcast_minimum_fusion.target_hbm
  1.7 0.1 select_reduce_fusion.2
  1.8 0.2 convert_reduce_fusion
  2.0 0.3 select_reduce_fusion.1
  2.3 0.6 pad_add_fusion.table_hbm
  2.9 0.0 copy-start
  2.9 1.6 %copy-done = bf16[512,2048]{1,0:T(8,128)(2,1)S(1)} copy-done((bf16[512,2048]{1,0:T(8,128)(2,1)S(1)}, bf16[512,2048]{1,0:T(8,128)(2,1)}, u32[]{:S(2)}) %copy-start) | copy-done | bytes 2097176
  4.5 0.0 copy-start.2
  4.5 1.0 copy-done.2
  5.6 0.0 copy-start.3
  5.6 0.7 copy-done.3
  6.2 46.8 %gather_amps.1 = (bf16[32,512,128]{2,1,0:T(8,128)(2,1)}, f32[4,512,128]{2,1,0:T(8,128)S(1)}) custom-call(s32[1,4]{1,0:T(1,128)S(1)} %copy-done.3, bf16[512,512]{1,0:T(8,128)(2,1)S(1)} %copy-done.2, bf16[512,2048]{1,0:T(8,128)(2,1)S(1)} %copy-done), custom_call_target="tpu_custom_call" | custom-call | tf_op jit(solution)/shard_map/gather_amps/pallas_call | solution.py:313
  53.0 0.0 copy-start.1
  53.1 1.0 copy-done.1
  54.0 0.0 copy-done.4
  54.0 23.1 %ladder_partial.1.part_ref = f32[32,512,128]{2,1,0:T(8,128)} custom-call(s32[2,416]{1,0:T(2,128)} %pad_add_fusion.table_hbm, s32[104]{0:T(128)} %broadcast_minimum_fusion.target_hbm, s32[32]{0:T(128)} %copy-done.4, bf16[32,512,128]{2,1,0:T(8,128)(2,1)} %get-tuple-element.8.amps_hbm, bf16[320,128,128]{2,1,0:T(8,128)(2,1)} %ints_hbm.1), custom_call_target="tpu_custom_call" | custom-call | tf_op jit(solution)/shard_map/ladder_partial/pallas_call | solution.py:336
  77.2 49.8 %reduce_partial.1 = f32[512,512]{1,0:T(8,128)} custom-call(s32[1,4]{1,0:T(1,128)} %keep_ref.1, f32[4,512,128]{2,1,0:T(8,128)} %copy-done.1, f32[32,512,128]{2,1,0:T(8,128)} %ladder_partial.1.part_ref), custom_call_target="tpu_custom_call" | custom-call | tf_op jit(solution)/shard_map/reduce_partial/pallas_call | solution.py:355
  127.0 2.3 %copy.8 = f32[512,512]{1,0:T(8,128)} copy(f32[512,512]{1,0:T(8,128)} %reduce_partial.1) | data formatting | bytes 2097152
  (3 shorter events, 0.0 us)
Async XLA Ops:
  1.0 53.0 %copy-start.4 = (s32[32]{0:T(128)}, s32[32]{0:T(128)S(1)}, u32[]{:S(2)}) copy-start(s32[32]{0:T(128)S(1)} %select_reduce_fusion.3.ends_hbm) | copy-start | bytes 388
  2.9 1.6 %copy-start = (bf16[512,2048]{1,0:T(8,128)(2,1)S(1)}, bf16[512,2048]{1,0:T(8,128)(2,1)}, u32[]{:S(2)}) copy-start(bf16[512,2048]{1,0:T(8,128)(2,1)} %w_hbm.1) | copy-start | bytes 6291460
  4.5 1.0 copy-start.2
  5.6 0.7 copy-start.3
  53.0 1.0 copy-start.1

commit v4 on v2

--- a/solution.py
+++ b/solution.py
@@ -10,8 +10,8 @@
 MESH = pl.DeviceIdType.MESH
 QROWS = 64
 QMAX = 32766.0
-GROUP = 4
-UNROLL = 4
+GROUP = 2
+UNROLL = 8
 PHASE = 4
 F32 = jnp.float32
 

time: 129 us -> 128 us (level)
    pallas_call x1, Pallas kernels: 24.6 us -> 23.1 us  [local(): pl.pallas_call(ladder_kernel, out_shape=jax.ShapeDtypeStruct((tiles_all,...]
where the time goes in v4:
time: 128 us
  Pallas kernels  118 us (92%)
  local copies, waits for them, and re-layouts  7.3 us (6%)
  other arithmetic  2.04 us (2%)
    pallas_call x1, Pallas kernels, local(): pl.pallas_call(functools.partial(reduce_kernel, n, pairs, tiles), out_sha...  48.1 us
    pallas_call x1, Pallas kernels, local(): pl.pallas_call(functools.partial(gather_kernel, n, pairs, tiles), out_sha...  46.9 us
    pallas_call x1, Pallas kernels, local(): pl.pallas_call(ladder_kernel, out_shape=jax.ShapeDtypeStruct((tiles_all,...  23.1 us
    unnamed x11, local copies, waits for them, and re-layouts  6.52 us

profile of v4, /device:TPU:0, one launch (start us, length us, event | category | flops | bytes accessed | tf_op | source)
XLA Modules:
  0.0 127.5 jit_solution(480988282268730314)
XLA Ops:
  0.0 0.8 slice_reduce_fusion.1
  0.8 0.1 convert_reduce_fusion.1
  0.9 0.1 select_reduce_fusion.3.ends_ref
  1.0 0.0 copy-start.4
  1.0 0.1 convert_reduce_fusion.2
  1.1 0.6 broadcast_minimum_fusion.target_ref
  1.7 0.1 select_reduce_fusion.2
  1.8 0.2 convert_reduce_fusion
  2.0 0.2 select_reduce_fusion.1
  2.3 0.6 pad_add_fusion.table_ref
  2.9 0.0 copy-start
  2.9 1.6 %copy-done = bf16[512,2048]{1,0:T(8,128)(2,1)S(1)} copy-done((bf16[512,2048]{1,0:T(8,128)(2,1)S(1)}, bf16[512,2048]{1,0:T(8,128)(2,1)}, u32[]{:S(2)}) %copy-start) | copy-done | bytes 2097176
  4.5 0.0 copy-start.2
  4.5 1.0 copy-done.2
  5.5 0.0 copy-start.3
  5.5 0.7 copy-done.3
  6.2 46.9 %gather_amps.1 = (bf16[32,512,128]{2,1,0:T(8,128)(2,1)}, f32[4,512,128]{2,1,0:T(8,128)S(1)}) custom-call(s32[1,4]{1,0:T(1,128)S(1)} %copy-done.3, bf16[512,512]{1,0:T(8,128)(2,1)S(1)} %copy-done.2, bf16[512,2048]{1,0:T(8,128)(2,1)S(1)} %copy-done), custom_call_target="tpu_custom_call" | custom-call | tf_op jit(solution)/shard_map/gather_amps/pallas_call | solution.py:306
  53.0 0.0 copy-start.1
  53.0 1.0 copy-done.1
  54.0 0.0 copy-done.4
  54.0 23.1 %ladder_partial.1.part_ref = f32[32,512,128]{2,1,0:T(8,128)} custom-call(s32[2,352]{1,0:T(2,128)} %pad_add_fusion.table_ref, s32[176]{0:T(256)} %broadcast_minimum_fusion.target_ref, s32[32]{0:T(128)} %copy-done.4, bf16[32,512,128]{2,1,0:T(8,128)(2,1)} %get-tuple-element.8.amps_hbm, bf16[320,128,128]{2,1,0:T(8,128)(2,1)} %ints_hbm.1), custom_call_target="tpu_custom_call" | custom-call | tf_op jit(solution)/shard_map/ladder_partial/pallas_call | solution.py:329
  77.1 48.1 %reduce_partial.1 = f32[512,512]{1,0:T(8,128)} custom-call(s32[1,4]{1,0:T(1,128)} %keep_ref.1, f32[4,512,128]{2,1,0:T(8,128)} %copy-done.1, f32[32,512,128]{2,1,0:T(8,128)} %ladder_partial.1.part_ref), custom_call_target="tpu_custom_call" | custom-call | tf_op jit(solution)/shard_map/reduce_partial/pallas_call | solution.py:345
  125.3 2.3 %copy.8 = f32[512,512]{1,0:T(8,128)} copy(f32[512,512]{1,0:T(8,128)} %reduce_partial.1) | data formatting | bytes 2097152
  (5 shorter events, 0.0 us)
Async XLA Ops:
  1.0 53.0 %copy-start.4 = (s32[32]{0:T(128)}, s32[32]{0:T(128)S(1)}, u32[]{:S(2)}) copy-start(s32[32]{0:T(128)S(1)} %select_reduce_fusion.3.ends_ref) | copy-start | bytes 388
  2.9 1.6 %copy-start = (bf16[512,2048]{1,0:T(8,128)(2,1)S(1)}, bf16[512,2048]{1,0:T(8,128)(2,1)}, u32[]{:S(2)}) copy-start(bf16[512,2048]{1,0:T(8,128)(2,1)} %w_hbm.1) | copy-start | bytes 6291460
  4.5 1.0 copy-start.2
  5.5 0.7 copy-start.3
  53.0 1.0 copy-start.1
